TPU v7x, 512 devices: a whole 4x4x16 slice. The times are simulated.
512 devices in a mesh: ctx: 32 (over x, y, core), exp: 16 (over z).
Axes of the slice: x: 4, y: 4, z: 16, core: 2. Of those that a mesh axis runs over, the one named last changes fastest.
Arguments:
- queries: bfloat16 [8192, 4096], P('ctx', 'exp'), may hold values from -6 to 6
- keys: bfloat16 [8192, 512], P('ctx'), may hold values from -6 to 6
- values: bfloat16 [8192, 512], P('ctx'), may hold values from -6 to 6
- out_proj: bfloat16 [4096, 2048], P('exp'), may hold values from -0.09375 to 0.09375
- resid: bfloat16 [8192, 2048], P('ctx'), may hold values from -12 to 12
- norm_gain: float32 [2048], replicated, may hold values from 0.1 to 1.9
- routes: int32 [8192, 8], P('ctx'), may hold values from 0 to 15, all different within a row; in each aligned block of 16 rows (0 to 15, 16 to 31, ...) at most 12 rows name the same one
- gates: float32 [8192, 8], P('ctx'), may hold values from 0.05 to 1
- w_gate: bfloat16 [16, 2048, 768], P('exp', 'ctx'), may hold values from -0.125 to 0.125
- w_up: bfloat16 [16, 2048, 768], P('exp', 'ctx'), may hold values from -0.125 to 0.125
- w_down: bfloat16 [16, 768, 2048], P('exp', None, 'ctx'), may hold values from -0.21875 to 0.21875
Outputs:
- attn: bfloat16 [8192, 4096], P('ctx', 'exp')
- layer_out: bfloat16 [8192, 2048], P(('ctx', 'exp'))
Inputs may be any that keep to these rules, and one draw needn't show every extreme that they name: `routes`: each row names 8 different experts; in every aligned block of 16 rows no expert is named by more than 12 rows, a bound that some block reaches.
All inputs are finite; a program needn't handle non-finite values.
Results may differ from a plain program's by a relative error of at most 0.02.
Values may be sent and summed in bfloat16 or wider, within the bound.
A program may use at most 64 MiB of HBM per device.

v0:
```python
from functools import partial
import math

import jax
import jax.numpy as jnp
from jax import lax
from jax.sharding import PartitionSpec as P

D = 2048
QUERY_HEADS = 32
KEY_VALUE_HEADS = 4
HEAD_SIZE = 128
EXPERTS = 16


NEG = -1e30


def softmax_update(state, scores, values_piece):
    peak, mass, accum = state
    new_peak = jnp.maximum(peak, jnp.max(scores, axis=2))
    weights = jnp.exp(scores - new_peak[:, :, None])
    mass = jnp.sum(weights, axis=2)
    accum = jnp.einsum(
        "hrk,kd->hrd",
        weights.astype(jnp.bfloat16),
        values_piece,
        preferred_element_type=jnp.float32,
    )
    return (new_peak, mass, accum)


def visit_half(state, query_half, spots, keys_piece, key_spots, values_piece, scale):
    scores = (
        jnp.einsum("rhd,kd->hrk", query_half, keys_piece, preferred_element_type=jnp.float32)
        * scale
    )
    allowed = key_spots[None, None, :] <= spots[None, :, None]
    scores = jnp.where(allowed, scores, NEG)
    return softmax_update(state, scores, values_piece)


def keep_state(state):
    return state


def attention(query_rows, positions, key_head, value_head):
    row_count, head_count, head_dim = query_rows.shape
    middle = row_count // 2
    scale = 1.0 / math.sqrt(head_dim)
    halves = (query_rows[:middle], query_rows[middle:])
    spots = (positions[:middle], positions[middle:])
    latest = (positions[middle - 1], positions[row_count - 1])
    blank = (
        jnp.full((head_count, middle), NEG, jnp.float32),
        jnp.zeros((head_count, middle), jnp.float32),
        jnp.zeros((head_count, middle, head_dim), jnp.float32),
    )
    carry = (blank, blank)
    start = jnp.int32(0)
    keys_piece = lax.all_gather(key_head, "ctx", axis=0, tiled=True)
    values_piece = lax.all_gather(value_head, "ctx", axis=0, tiled=True)
    key_spots = jnp.arange(keys_piece.shape[0], dtype=jnp.int32)
    updated = []
    for which in range(2):
        visit = partial(
            visit_half,
            query_half=halves[which],
            spots=spots[which],
            keys_piece=keys_piece,
            key_spots=key_spots,
            values_piece=values_piece,
            scale=scale,
        )
        updated.append(lax.cond(start <= latest[which], visit, keep_state, carry[which]))
    result = (updated[0], updated[1])
    pieces = [state[2] / state[1][:, :, None] for state in result]
    joined = jnp.concatenate(pieces, axis=1)
    return (
        jnp.transpose(joined, (1, 0, 2))
        .reshape(row_count, head_count * head_dim)
        .astype(jnp.bfloat16)
    )


def expert_whole(rows_in, w_gate, w_up, w_down):
    gate_sum = jnp.einsum(
        "erd,edf->erf",
        rows_in,
        lax.all_gather(w_gate, "ctx", axis=1, tiled=True),
        preferred_element_type=jnp.float32,
    )
    up_sum = jnp.einsum(
        "erd,edf->erf",
        rows_in,
        lax.all_gather(w_up, "ctx", axis=1, tiled=True),
        preferred_element_type=jnp.float32,
    )
    act = (jax.nn.silu(gate_sum) * up_sum).astype(jnp.bfloat16)
    return jnp.einsum(
        "erf,efd->erd",
        act,
        lax.all_gather(w_down, "ctx", axis=2, tiled=True),
        preferred_element_type=jnp.float32,
    ).astype(jnp.bfloat16)


def block_ranks(route_rows, block_rows):
    count, top = route_rows.shape
    flat = route_rows.reshape(count * top)
    onehot = (flat[:, None] == jnp.arange(EXPERTS, dtype=jnp.int32)[None, :]).astype(jnp.int32)
    grouped = onehot.reshape(count // block_rows, block_rows * top, EXPERTS)
    before = (jnp.cumsum(grouped, axis=1, dtype=jnp.int32) - grouped).reshape(count * top, EXPERTS)
    rank = jnp.sum(before * onehot, axis=1)
    block_of = jnp.arange(count * top, dtype=jnp.int32) // (block_rows * top)
    return (flat, rank, block_of)


def normalize(hidden, norm_gain):
    return (
        hidden * lax.rsqrt(jnp.mean(hidden * hidden, axis=1, keepdims=True) + 1e-06) * norm_gain
    ).astype(jnp.bfloat16)


def local(queries, keys, values, out_proj, resid, norm_gain, routes, gates, w_gate, w_up, w_down):
    token_count, local_width = queries.shape
    head_count = local_width // HEAD_SIZE
    context_index = lax.axis_index("ctx")
    expert_number = lax.axis_index("exp")
    expert_devices = lax.axis_size("exp")
    shared_key_head = expert_number * head_count // (QUERY_HEADS // KEY_VALUE_HEADS)
    key_head = lax.dynamic_slice_in_dim(keys, shared_key_head * HEAD_SIZE, HEAD_SIZE, 1)
    value_head = lax.dynamic_slice_in_dim(values, shared_key_head * HEAD_SIZE, HEAD_SIZE, 1)
    positions = context_index * token_count + jnp.arange(token_count, dtype=jnp.int32)
    attn = attention(
        queries.reshape(token_count, head_count, HEAD_SIZE), positions, key_head, value_head
    )
    own_count = token_count // expert_devices
    top = routes.shape[1]
    capacity = own_count * top * 3 // (2 * EXPERTS)
    local_experts = w_gate.shape[0]
    share_all = gates / jnp.sum(gates, axis=1, keepdims=True)
    term = jnp.dot(attn, out_proj, preferred_element_type=jnp.float32)
    proj = lax.psum(term.astype(jnp.bfloat16), "exp").astype(jnp.float32)
    hidden_all = resid.astype(jnp.float32) + proj
    normed = normalize(hidden_all, norm_gain)
    flat, rank, block_of = block_ranks(routes, own_count)
    local_index = flat - expert_number * local_experts
    inside = (local_index >= 0) & (local_index < local_experts)
    place = jnp.where(
        inside, local_index * (expert_devices * capacity) + block_of * capacity + rank, -1
    ).reshape(token_count, top)
    places = jnp.arange(local_experts * expert_devices * capacity, dtype=jnp.int32)
    dispatch_table = jnp.any(places[:, None, None] == place[None, :, :], axis=2).astype(
        jnp.bfloat16
    )
    gathered = jnp.dot(dispatch_table, normed, preferred_element_type=jnp.float32).astype(
        jnp.bfloat16
    )
    rows_in = gathered.reshape(local_experts, expert_devices * capacity, D)
    expert_out = expert_whole(rows_in, w_gate, w_up, w_down)
    combine_table = jnp.zeros((token_count, places.shape[0]), jnp.float32)
    for route in range(top):
        combine_table = combine_table + jnp.where(
            place[:, route][:, None] == places[None, :], share_all[:, route][:, None], 0.0
        )
    flat_out = expert_out.reshape(places.shape[0], D).astype(jnp.float32)
    contribution = jnp.dot(combine_table, flat_out, precision=lax.Precision.HIGHEST)
    mixture = lax.psum_scatter(
        contribution.astype(jnp.bfloat16), "exp", scatter_dimension=0, tiled=True
    ).astype(jnp.float32)
    own_hidden = lax.dynamic_slice_in_dim(hidden_all, expert_number * own_count, own_count, 0)
    layer_out = (own_hidden + mixture).astype(jnp.bfloat16)
    return (attn, layer_out)


def solution(mesh):
    placed = (
        P("ctx", "exp"),
        P("ctx", None),
        P("ctx", None),
        P("exp", None),
        P("ctx", None),
        P(),
        P("ctx", None),
        P("ctx", None),
        P("exp", "ctx", None),
        P("exp", "ctx", None),
        P("exp", None, "ctx"),
    )
    return jax.shard_map(
        local,
        mesh=mesh,
        in_specs=placed,
        out_specs=(P("ctx", "exp"), P(("ctx", "exp"), None)),
        check_vma=False,
    )
```

profile of v0, /device:TPU:6, one launch (start us, length us, event | category | flops | bytes accessed | tf_op | source)
XLA Modules:
  0.0 574.9 jit_solution(10243876489296554421)
XLA Ops:
  7.2 1.6 constant_dynamic-slice_fusion.1
  8.9 1.5 constant_dynamic-slice_fusion
  10.4 0.6 fusion.94
  12.3 62.6 %all-gather.6.cloned.1.call-done = bf16[8192,128]{1,0:T(8,128)(2,1)} async-done(((bf16[256,128]{1,0:T(8,128)(2,1)}), bf16[8192,128]{1,0:T(8,128)(2,1)}) %all-gather.6.cloned.1.call-update) | async-done | bytes 2097168 | tf_op jit(solution)/shard_map/all_gather | solution.py:61
  74.9 62.2 %all-gather.8.cloned.1.call-done = bf16[8192,128]{1,0:T(8,128)(2,1)} async-done(((bf16[256,128]{1,0:T(8,128)(2,1)}), bf16[8192,128]{1,0:T(8,128)(2,1)}) %all-gather.8.cloned.1.call-update) | async-done | bytes 2097168 | tf_op jit(solution)/shard_map/all_gather | solution.py:62
  137.1 11.0 %conditional.2 = (f32[2,128]{1,0:T(2,128)S(1)}, f32[2,128,128]{2,1,0:T(8,128)S(1)}) conditional(s32[]{:T(128)} %bitcast.8, () %tuple.24, (s32[8192]{0:T(1024)S(1)}, s32[256]{0:T(256)S(1)}, bf16[256,256]{1,0:T(8,128)(2,1)}, bf16[8192,128]{1,0:T(8,128)(2,1)}, bf16[8192,128]{1,0:T(8,128)(2,1)}) %tuple.28), branch_computations={%region_0.1_spmd, %region_1.4_spmd} | conditional | flops 1089470208 | bytes 40476204 | solution.py:75
  137.1 3.7 broadcast_compare_fusion
  140.8 1.0 copy.64
  141.8 3.5 fusion.90
  145.4 1.6 fusion.4
  147.0 1.1 fusion.3
  148.1 11.1 %conditional.3 = (f32[2,128]{1,0:T(2,128)S(1)}, f32[2,128,128]{2,1,0:T(8,128)S(1)}) conditional(s32[]{:T(128)} %bitcast.9, () %tuple.26, (s32[8192]{0:T(1024)S(1)}, s32[256]{0:T(256)S(1)}, bf16[256,256]{1,0:T(8,128)(2,1)}, bf16[8192,128]{1,0:T(8,128)(2,1)}, bf16[8192,128]{1,0:T(8,128)(2,1)}) %tuple.28), branch_computations={%region_4.5_spmd, %region_5.8_spmd} | conditional | flops 1089470208 | bytes 40476204 | solution.py:75
  148.1 3.7 broadcast_compare_fusion.1
  151.9 1.0 copy.65
  152.9 3.5 fusion.91
  156.4 1.6 fusion.13
  158.1 1.1 fusion.12
  159.4 1.4 convolution_convert_fusion.1
  161.5 0.5 all-gather.12.cloned.1.call-update
  163.2 2.8 select_reduce_fusion
  166.3 0.6 fusion.27
  166.9 132.8 %all-reduce.2.cloned.1.call-done = bf16[256,2048]{1,0:T(8,128)(2,1)} async-done(((bf16[256,2048]{1,0:T(8,128)(2,1)}), bf16[256,2048]{1,0:T(8,128)(2,1)}) %all-reduce.2.cloned.1.call-update) | async-done | bytes 1048592 | tf_op jit(solution)/shard_map/psum | solution.py:144
  299.6 2.0 convert_add_fusion
  301.7 2.8 convolution_convert_fusion.2
  304.5 55.1 %all-gather.10.cloned.1.call-done = bf16[1,2048,768]{2,1,0:T(8,128)(2,1)} async-done(((bf16[1,64,768]{2,1,0:T(8,128)(2,1)}), bf16[1,2048,768]{2,1,0:T(8,128)(2,1)}) %all-gather.10.cloned.1.call-update) | async-done | bytes 3145744 | tf_op jit(solution)/shard_map/all_gather | solution.py:90
  359.6 3.8 fusion.22
  363.4 59.6 %all-gather.12.cloned.1.call-done = bf16[1,2048,768]{2,1,0:T(8,128)(2,1)} async-done(((bf16[1,64,768]{2,1,0:T(8,128)(2,1)}), bf16[1,2048,768]{2,1,0:T(8,128)(2,1)}) %all-gather.12.cloned.1.call-update) | async-done | bytes 3145744 | tf_op jit(solution)/shard_map/all_gather | solution.py:96
  422.9 63.3 %all-gather.14.cloned.1.call-done = bf16[1,768,2048]{1,2,0:T(8,128)(2,1)} async-done(((bf16[1,768,64]{1,2,0:T(8,128)(2,1)}), bf16[1,768,2048]{1,2,0:T(8,128)(2,1)}) %all-gather.14.cloned.1.call-update) | async-done | bytes 3145744 | tf_op jit(solution)/shard_map/all_gather | solution.py:103
  486.3 6.1 %fusion.24 = bf16[192,2048]{1,0:T(8,128)(2,1)} fusion(bf16[1,768,2048]{1,2,0:T(8,128)(2,1)} %all-gather.14.cloned.1.call-done, bf16[192,2048]{1,0:T(8,128)(2,1)} %convolution_convert_fusion.2, bf16[1,2048,768]{2,1,0:T(8,128)(2,1)} %all-gather.12.cloned.1.call-done, f32[192,768]{1,0:T(8,128)} %fusion.22), kind=kOutput, calls=%fused_computation.32 | convolution fusion | flops 1209237504 | bytes 8454144 | tf_op jit(solution)/shard_map/erf,efd->erd/dot_general | solution.py:100
  492.4 3.7 convolution_convert_fusion
  496.1 70.5 %reduce-scatter.2.cloned.1.call-done = bf16[16,2048]{1,0:T(8,128)(2,1)} async-done(((bf16[256,2048]{1,0:T(8,128)(2,1)}), bf16[16,2048]{1,0:T(8,128)(2,1)}) %reduce-scatter.2.cloned.1.call-update) | async-done | bytes 65552 | tf_op jit(solution)/shard_map/reduce_scatter | solution.py:169
  566.6 1.5 add_convert_fusion
  (51 shorter events, 2.4 us)
Async XLA Ops:
  7.2 152.2 %copy-start = (bf16[256,2048]{1,0:T(8,128)(2,1)S(1)}, bf16[256,2048]{1,0:T(8,128)(2,1)}, u32[]{:S(2)}) copy-start(bf16[256,2048]{1,0:T(8,128)(2,1)} %param.18) | copy-start | bytes 3145732
  7.2 67.7 %all-gather.6.cloned.1.call-start = ((), (), s32[]{:S(2)}) async-start(), calls=%async_computation.1 | async-start | bytes 2162688 | tf_op jit(solution)/shard_map/all_gather | solution.py:61
  8.8 128.2 %all-gather.8.cloned.1.call-start = ((), (), s32[]{:S(2)}) async-start(), calls=%async_computation.2 | async-start | bytes 2162688 | tf_op jit(solution)/shard_map/all_gather | solution.py:62
  10.4 289.2 %all-reduce.2.cloned.1.call-start = ((), (), s32[]{:S(2)}) async-start(), calls=%async_computation.3 | async-start | bytes 2097152 | tf_op jit(solution)/shard_map/psum | solution.py:144
  141.8 3.5 copy-start.1
  152.9 3.5 copy-start.2
  159.2 3.6 copy-start.5
  159.2 7.0 %copy-start.6 = (f32[256,8]{0,1:T(8,128)S(1)}, f32[256,8]{0,1:T(8,128)}, u32[]{:S(2)}) copy-start(f32[256,8]{0,1:T(8,128)} %param.22) | copy-start | bytes 24580
  159.4 142.3 %copy-start.4 = (bf16[256,256]{1,0:T(8,128)(2,1)}, bf16[256,256]{1,0:T(8,128)(2,1)S(1)}, u32[]{:S(2)}) copy-start(bf16[256,256]{1,0:T(8,128)(2,1)S(1)} %copy_bitcast_fusion) | copy-start | bytes 393220
  160.8 140.9 %copy-start.7 = (f32[2048]{0:T(1024)S(1)}, f32[2048]{0:T(1024)}, u32[]{:S(2)}) copy-start(f32[2048]{0:T(1024)} %param.20) | copy-start | bytes 24580
  160.8 198.7 %all-gather.10.cloned.1.call-start = ((), (), s32[]{:S(2)}) async-start(), calls=%async_computation.4 | async-start | bytes 3244032 | tf_op jit(solution)/shard_map/all_gather | solution.py:90
  161.4 261.5 %all-gather.12.cloned.1.call-start = ((), (), s32[]{:S(2)}) async-start(), calls=%async_computation.5 | async-start | bytes 3244032 | tf_op jit(solution)/shard_map/all_gather | solution.py:96
  162.0 324.2 %all-gather.14.cloned.1.call-start = ((), (), s32[]{:S(2)}) async-start(), calls=%async_computation.6 | async-start | bytes 3244032 | tf_op jit(solution)/shard_map/all_gather | solution.py:103
  162.6 404.0 %reduce-scatter.2.cloned.1.call-start = ((), (), s32[]{:S(2)}) async-start(), calls=%async_computation.7 | async-start | bytes 1114112 | tf_op jit(solution)/shard_map/reduce_scatter | solution.py:169
  299.6 2.1 copy-start.3
Sparse Core Ops, SparseCore 0:
  11.7 63.0 all-gather.5
  78.6 58.4 all-gather.7
  161.0 138.6 all-reduce.1
  303.1 56.4 all-gather.9
  363.0 59.8 all-gather.11
  426.4 59.8 all-gather.13
  496.2 70.3 reduce-scatter.1
where the time goes:
time: 575 us
  waiting for transfers between devices  508 us (88%)
  matrix products  28 us (5%)
  other arithmetic  16.7 us (3%)
  between operations  15.6 us (3%)
  local copies, waits for them, and re-layouts  6.3 us (1%)
    psum x1, waiting for transfers between devices, local(): proj = lax.psum(term.astype(jnp.bfloat16), 'exp').astype(jnp.float32)  133 us
    reduce_scatter x1, waiting for transfers between devices, local(): lax.psum_scatter(contribution.astype(jnp.bfloat16), 'exp', scatter_dimens...  70.5 us
    all_gather x1, waiting for transfers between devices, expert_whole(): lax.all_gather(w_down, 'ctx', axis=2, tiled=True)  63.3 us
    all_gather x1, waiting for transfers between devices, attention(): keys_piece = lax.all_gather(key_head, 'ctx', axis=0, tiled=True)  62.6 us
    all_gather x1, waiting for transfers between devices, attention(): values_piece = lax.all_gather(value_head, 'ctx', axis=0, tiled=True)  62.2 us
    all_gather x1, waiting for transfers between devices, expert_whole(): lax.all_gather(w_up, 'ctx', axis=1, tiled=True)  59.6 us
    all_gather x1, waiting for transfers between devices, expert_whole(): lax.all_gather(w_gate, 'ctx', axis=1, tiled=True)  55.1 us
  transfers between devices with their start and end apart: 7, of which 7 were waited for; matrix products, arithmetic and copies ran while one was open for 3% of the time, Pallas kernels for 0%

commit v1 on v0

v1 whole, which is shorter than its diff:
```python
import math

import jax
import jax.numpy as jnp
from jax import lax
from jax.experimental import pallas as pl
from jax.experimental.pallas import tpu as pltpu
from jax.sharding import PartitionSpec as P

D = 2048
FF = 768
HEAD_SIZE = 128
KEY_HEAD_SHARERS = 4
SIDE = 4
RING = 16
TOKENS = 256
OWN = 16
HALF = D // 2
BLOCK = 1024
NEG = -1e30
F32 = jnp.float32
BF16 = jnp.bfloat16
MESH = pl.DeviceIdType.MESH


def wrap(index, size):
    return lax.rem(index + size, jnp.int32(size))


def remote(src, dst, sends, recvs, index, device):
    return pltpu.make_async_remote_copy(
        src_ref=src,
        dst_ref=dst,
        send_sem=sends.at[index],
        recv_sem=recvs.at[index],
        device_id=device,
        device_id_type=MESH,
    )


class TorusGather:
    def __init__(self, buf, sends, recvs, spot, devices, cut):
        first, second, core = spot
        to_first, to_second, to_core = devices
        up, down = wrap(first + 1, SIDE), wrap(first - 1, SIDE)
        above, below = wrap(second + 1, SIDE), wrap(second - 1, SIDE)
        across = wrap(second + 2, SIDE)
        size = buf.shape[3]
        own = buf.at[first, second, core]
        head = buf.at[down, second, core, pl.ds(0, cut)]
        tail = buf.at[up, second, core, pl.ds(cut, size - cut)]
        row = buf.at[:, second, core]
        row_head = buf.at[pl.ds(0, 2), below, core]
        row_tail = buf.at[pl.ds(2, 2), above, core]
        plan = [
            (own, to_first(up)),
            (own, to_first(down)),
            (head, to_first(up)),
            (tail, to_first(down)),
            (row, to_second(above)),
            (row, to_second(below)),
            (row_head, to_second(above)),
            (row_tail, to_second(below)),
            (row, to_core),
            (buf.at[:, below, core], to_core),
            (buf.at[:, above, core], to_core),
            (buf.at[:, across, core], to_core),
        ]
        self.copies = [
            remote(ref, ref, sends, recvs, index, device) for index, (ref, device) in enumerate(plan)
        ]

    def start(self, *which):
        for index in which:
            self.copies[index].start()

    def arrive(self, *which):
        for index in which:
            self.copies[index].wait_recv()

    def drain(self):
        for copy in self.copies:
            copy.wait_send()


class RingScatter:
    def __init__(self, terms, ring, sends, recvs, place):
        self.terms, self.ring, self.sends, self.recvs, self.place = terms, ring, sends, recvs, place
        self.next = ({"exp": wrap(place + 1, RING)}, {"exp": wrap(place - 1, RING)})

    def copy(self, way, step, half, src=None):
        src = self.ring.at[way, step, half] if src is None else src
        return remote(
            src,
            self.ring.at[way, step + 1, half],
            self.sends,
            self.recvs,
            (way, step, half),
            self.next[way],
        )

    def owner(self, way, step):
        return wrap(self.place + RING // 2 - step if way == 0 else self.place - RING // 2 + 1 + step, RING)

    def begin(self, half):
        for way in range(2):
            self.copy(way, 0, half, self.terms.at[self.owner(way, 0), half]).start()

    def advance(self, way, step, half):
        self.copy(way, step - 1, half).wait_recv()
        total = self.ring[way, step, half].astype(F32) + self.terms[self.owner(way, step), half].astype(F32)
        self.ring[way, step, half] = total.astype(BF16)
        self.copy(way, step, half).start()

    def run(self):
        def step(index, _):
            for half in range(2):
                for way in range(2):
                    self.advance(way, index, half)
            return 0

        lax.fori_loop(1, RING // 2 - 1, step, 0)
        for half in range(2):
            self.advance(0, RING // 2 - 1, half)

    def total(self, half):
        self.copy(0, RING // 2 - 1, half).wait_recv()
        self.copy(1, RING // 2 - 2, half).wait_recv()
        own = self.terms[self.place, half].astype(F32)
        return own + self.ring[0, RING // 2, half].astype(F32) + self.ring[1, RING // 2 - 1, half].astype(F32)

    def drain(self):
        def step(index, _):
            for half in range(2):
                for way in range(2):
                    self.copy(way, index, half).wait_send()
            return 0

        lax.fori_loop(0, RING // 2 - 1, step, 0)
        for half in range(2):
            self.copy(0, RING // 2 - 1, half).wait_send()


class RingGather:
    def __init__(self, rows, sends, recvs, place):
        self.rows, self.sends, self.recvs, self.place = rows, sends, recvs, place
        self.next = ({"exp": wrap(place + 1, RING)}, {"exp": wrap(place - 1, RING)})

    def copy(self, way, step, half):
        origin = wrap(self.place - step if way == 0 else self.place + step, RING)
        ref = self.rows.at[origin, half]
        return remote(ref, ref, self.sends, self.recvs, (way, step, half), self.next[way])

    def begin(self, half):
        for way in range(2):
            self.copy(way, 0, half).start()

    def run(self):
        def step(index, _):
            for half in range(2):
                for way in range(2):
                    self.copy(way, index - 1, half).wait_recv()
                    self.copy(way, index, half).start()
            return 0

        lax.fori_loop(1, RING // 2 - 1, step, 0)
        for half in range(2):
            self.copy(0, RING // 2 - 2, half).wait_recv()
            self.copy(0, RING // 2 - 1, half).start()
        for half in range(2):
            self.copy(1, RING // 2 - 2, half).wait_recv()
            self.copy(0, RING // 2 - 1, half).wait_recv()

    def drain(self):
        def step(index, _):
            for half in range(2):
                for way in range(2):
                    self.copy(way, index, half).wait_send()
            return 0

        lax.fori_loop(0, RING // 2 - 1, step, 0)
        for half in range(2):
            self.copy(0, RING // 2 - 1, half).wait_send()


def nt_dot(left, right):
    return lax.dot_general(left, right, (((1,), (1,)), ((), ())), preferred_element_type=F32)


def dot(left, right):
    return jnp.dot(left, right, preferred_element_type=F32)


def layer(
    queries, keys, values, out_proj, resid, gain, routes, gates, w_gate, w_up, w_down,
    attn_out, layer_out,
    kbuf, vbuf, abuf, bbuf, q_v, proj_v, resid_v, gain_v, routes_v, gates_v, weight_v, attn_v, hidden_v,
    terms, ring_one, normed, mixed, ring_two,
    loads, kv_sends, kv_recvs, w_sends, w_recvs, z_sends, z_recvs,
):
    ctx, place = lax.axis_index("ctx"), lax.axis_index("exp")
    x, y, core = lax.div(ctx, 8), lax.rem(lax.div(ctx, 2), 4), lax.rem(ctx, 2)

    def to_x(index):
        return {"ctx": index * 8 + y * 2 + core}

    def to_y(index):
        return {"ctx": x * 8 + index * 2 + core}

    to_core = {"ctx": x * 8 + y * 2 + (1 - core)}
    x_first = ((x, y, core), (to_x, to_y, to_core))
    y_first = ((y, x, core), (to_y, to_x, to_core))

    head_columns = pl.ds(pl.multiple_of(lax.div(place, KEY_HEAD_SHARERS) * HEAD_SIZE, HEAD_SIZE), HEAD_SIZE)
    own_rows = pl.ds(pl.multiple_of(place * OWN, OWN), OWN)
    own_a, own_b = abuf.at[x, y, core], bbuf.at[y, x, core]
    pairs = [
        (keys.at[:, head_columns], kbuf.at[x, y, core]),
        (values.at[:, head_columns], vbuf.at[y, x, core]),
        (queries, q_v),
        (w_gate, own_a.at[pl.ds(0, 64)]),
        (w_down.at[pl.ds(0, 32)], own_a.at[pl.ds(64, 32)]),
        (w_up, own_b.at[pl.ds(0, 64)]),
        (w_down.at[pl.ds(32, 32)], own_b.at[pl.ds(64, 32)]),
        (out_proj, proj_v),
        (resid.at[own_rows], resid_v),
        (gain, gain_v),
        (routes, routes_v),
        (gates, gates_v),
    ]
    local = [pltpu.make_async_copy(src, dst, loads.at[i]) for i, (src, dst) in enumerate(pairs)]
    for copy in local:
        copy.start()

    barrier = pltpu.get_barrier_semaphore()
    neighbours = [
        to_x(wrap(x + 1, SIDE)), to_x(wrap(x - 1, SIDE)), to_y(wrap(y + 1, SIDE)), to_y(wrap(y - 1, SIDE)),
        to_core, {"exp": wrap(place + 1, RING)}, {"exp": wrap(place - 1, RING)},
    ]
    for device in neighbours:
        pl.semaphore_signal(barrier, inc=1, device_id=device, device_id_type=MESH)
    pl.semaphore_wait(barrier, len(neighbours))

    k_gather = TorusGather(kbuf, kv_sends.at[0], kv_recvs.at[0], *x_first, 128)
    v_gather = TorusGather(vbuf, kv_sends.at[1], kv_recvs.at[1], *y_first, 128)
    a_gather = TorusGather(abuf, w_sends.at[0], w_recvs.at[0], *x_first, 48)
    b_gather = TorusGather(bbuf, w_sends.at[1], w_recvs.at[1], *y_first, 48)
    heads, experts = (k_gather, v_gather), (a_gather, b_gather)

    for index, gather in enumerate(heads):
        local[index].wait()
        gather.start(0, 1)
    for gather in heads:
        gather.arrive(0)
        gather.start(2)
        gather.arrive(1)
        gather.start(3)
    for gather in heads:
        gather.arrive(2, 3)
        gather.start(4, 5, 8)
    for copy in local[2:]:
        copy.wait()
    for gather in experts:
        gather.start(0, 1)
    for gather in heads:
        gather.arrive(4)
        gather.start(6, 9)
        gather.arrive(5)
        gather.start(7, 10)

    all_gates = gates_v[...]
    share = all_gates / jnp.sum(all_gates, axis=0, keepdims=True)
    here = jnp.sum(jnp.where(routes_v[...] == place, share, 0.0), axis=0, keepdims=True)
    weight_v[...] = jnp.broadcast_to(here, (128, TOKENS)).T

    for gather in heads:
        gather.arrive(6, 7)
        gather.start(11)
    for gather in experts:
        gather.arrive(0)
        gather.start(2)
        gather.arrive(1)
        gather.start(3)
    for gather in heads:
        gather.arrive(8, 9, 10, 11)

    query = jnp.concatenate([q_v[:, :HEAD_SIZE], q_v[:, HEAD_SIZE:]], axis=0)
    scale = math.log2(math.e) / math.sqrt(HEAD_SIZE)
    offset = lax.rem(ctx, 4) * TOKENS

    def visit(index, state, masked=False):
        peak, mass, accum = state
        far, near = lax.div(index, 2), lax.rem(index, 2) * 2
        some_keys = kbuf[far, pl.ds(near, 2)].reshape(BLOCK, HEAD_SIZE)
        some_values = vbuf[pl.ds(near, 2), far].reshape(BLOCK, HEAD_SIZE)
        scores = nt_dot(query, some_keys)
        if masked:
            row = lax.broadcasted_iota(jnp.int32, scores.shape, 0) & (TOKENS - 1)
            column = lax.broadcasted_iota(jnp.int32, scores.shape, 1)
            scores = jnp.where(column <= row + offset, scores, NEG)
        new_peak = jnp.maximum(peak, jnp.max(scores, axis=1, keepdims=True))
        weights = jnp.exp2((scores - new_peak) * scale)
        fade = jnp.exp2((peak - new_peak) * scale)
        part = weights[:, :128]
        for low in range(128, BLOCK, 128):
            part = part + weights[:, low : low + 128]
        mass = mass * fade + part
        accum = accum * fade + dot(weights.astype(BF16), some_values)
        return (new_peak, mass, accum)

    last = lax.div(ctx, 4)
    middle = lax.div(last, 2)
    state = (
        jnp.full((2 * TOKENS, 1), NEG, F32),
        jnp.zeros((2 * TOKENS, 128), F32),
        jnp.zeros((2 * TOKENS, HEAD_SIZE), F32),
    )
    state = lax.fori_loop(0, middle, visit, state)
    for gather in experts:
        gather.arrive(2, 3)
        gather.start(4, 5, 8)
    state = lax.fori_loop(middle, last, visit, state)
    _, mass, accum = visit(last, state, masked=True)
    result = (accum / jnp.sum(mass, axis=1, keepdims=True)).astype(BF16)
    attn_v[:, :HEAD_SIZE] = result[:TOKENS]
    attn_v[:, HEAD_SIZE:] = result[TOKENS:]
    attn_copy = pltpu.make_async_copy(attn_v, attn_out, loads.at[len(pairs)])
    attn_copy.start()

    scatter_one = RingScatter(terms, ring_one, z_sends.at[0], z_recvs.at[0], place)
    for half in range(2):
        term = dot(attn_v[...], proj_v[:, half * HALF : (half + 1) * HALF])
        terms[:, half] = term.astype(BF16).reshape(RING, OWN, HALF)
        scatter_one.begin(half)
    for gather in experts:
        gather.arrive(4)
        gather.start(6, 9)
        gather.arrive(5)
        gather.start(7, 10)
    scatter_one.run()
    for half in range(2):
        columns = slice(half * HALF, (half + 1) * HALF)
        hidden_v[:, columns] = resid_v[:, columns].astype(F32) + scatter_one.total(half)

    hidden = hidden_v[...]
    spread = lax.rsqrt(jnp.mean(hidden * hidden, axis=1, keepdims=True) + 1e-06)
    rows = (hidden * spread * gain_v[...]).astype(BF16)
    spread_rows = RingGather(normed, z_sends.at[1], z_recvs.at[1], place)
    for half in range(2):
        normed[place, half] = rows[:, half * HALF : (half + 1) * HALF]
        spread_rows.begin(half)
    for gather in experts:
        gather.arrive(6, 7)
        gather.start(11)
    spread_rows.run()
    for gather in experts:
        gather.arrive(8, 9, 10, 11)

    gate_sum = jnp.zeros((TOKENS, FF), F32)
    for half in range(2):
        part = normed[:, half].reshape(TOKENS, HALF)
        gate_sum += dot(part, abuf[2 * half : 2 * half + 2, :, :, :64].reshape(HALF, FF))
    up_sum = jnp.zeros((TOKENS, FF), F32)
    for quarter in range(SIDE):
        low = quarter % 2 * 512
        part = normed[:, quarter // 2, :, low : low + 512].reshape(TOKENS, 512)
        up_sum += dot(part, bbuf[:, quarter, :, :64].reshape(512, FF))
    act = (gate_sum / (1.0 + jnp.exp(-gate_sum)) * up_sum).astype(BF16)
    weight = weight_v[:, :1]
    scatter_two = RingScatter(mixed, ring_two, z_sends.at[2], z_recvs.at[2], place)
    for quarter in range(SIDE):
        low = quarter % 2 * 512
        down = jnp.concatenate([abuf[quarter, :, :, 64:], bbuf[:, quarter, :, 64:]], axis=2)
        part = nt_dot(act, down.reshape(512, FF)).astype(BF16).astype(F32)
        part = jnp.where(weight > 0.0, weight * part, 0.0).astype(BF16)
        mixed[:, quarter // 2, :, low : low + 512] = part.reshape(RING, OWN, 512)
        if quarter % 2:
            scatter_two.begin(quarter // 2)
    scatter_two.run()
    for half in range(2):
        columns = slice(half * HALF, (half + 1) * HALF)
        layer_out[:, columns] = (hidden_v[:, columns] + scatter_two.total(half)).astype(BF16)

    attn_copy.wait()
    for gather in (*heads, *experts, scatter_one, spread_rows, scatter_two):
        gather.drain()


def local_layer(queries, keys, values, out_proj, resid, norm_gain, routes, gates, w_gate, w_up, w_down):
    anywhere = pl.BlockSpec(memory_space=pl.ANY)
    torus = (SIDE, SIDE, 2)
    pieces = (RING, 2, OWN, HALF)
    ring = (2, RING // 2 + 1, 2, OWN, HALF)
    ring_sems = pltpu.SemaphoreType.DMA((3, 2, RING // 2, 2))
    gather_sems = pltpu.SemaphoreType.DMA((2, 12))
    return pl.pallas_call(
        layer,
        out_shape=(
            jax.ShapeDtypeStruct(queries.shape, BF16),
            jax.ShapeDtypeStruct((OWN, D), BF16),
        ),
        in_specs=[anywhere] * 11,
        out_specs=(anywhere, pl.BlockSpec(memory_space=pltpu.VMEM)),
        scratch_shapes=[
            pltpu.VMEM((*torus, TOKENS, HEAD_SIZE), BF16),
            pltpu.VMEM((*torus, TOKENS, HEAD_SIZE), BF16),
            pltpu.VMEM((*torus, 96, FF), BF16),
            pltpu.VMEM((*torus, 96, FF), BF16),
            pltpu.VMEM(queries.shape, BF16),
            pltpu.VMEM(out_proj.shape, BF16),
            pltpu.VMEM((OWN, D), BF16),
            pltpu.VMEM((1, D), F32),
            pltpu.VMEM((8, TOKENS), jnp.int32),
            pltpu.VMEM((8, TOKENS), F32),
            pltpu.VMEM((TOKENS, 128), F32),
            pltpu.VMEM(queries.shape, BF16),
            pltpu.VMEM((OWN, D), F32),
            pltpu.VMEM(pieces, BF16),
            pltpu.VMEM(ring, BF16),
            pltpu.VMEM(pieces, BF16),
            pltpu.VMEM(pieces, BF16),
            pltpu.VMEM(ring, BF16),
            pltpu.SemaphoreType.DMA((13,)),
            gather_sems,
            gather_sems,
            gather_sems,
            gather_sems,
            ring_sems,
            ring_sems,
        ],
        compiler_params=pltpu.CompilerParams(
            collective_id=0, has_side_effects=True, vmem_limit_bytes=56 * 1024 * 1024
        ),
        name="layer",
    )(
        queries,
        keys,
        values,
        out_proj,
        resid,
        norm_gain.reshape(1, D),
        routes.T,
        gates.T,
        w_gate[0],
        w_up[0],
        w_down[0].T,
    )


def solution(mesh):
    placed = (
        P("ctx", "exp"),
        P("ctx", None),
        P("ctx", None),
        P("exp", None),
        P("ctx", None),
        P(),
        P("ctx", None),
        P("ctx", None),
        P("exp", "ctx", None),
        P("exp", "ctx", None),
        P("exp", None, "ctx"),
    )
    return jax.shard_map(
        local_layer,
        mesh=mesh,
        in_specs=placed,
        out_specs=(P("ctx", "exp"), P(("ctx", "exp"), None)),
        check_vma=False,
    )
```

time: 575 us -> 138 us (0.24)
  waiting for transfers between devices: 508 us -> 0 us
  Pallas kernels: 0 us -> 135 us
  matrix products: 28 us -> 0 us
  other arithmetic: 16.7 us -> 0 us
  between operations: 15.6 us -> 0.65 us
    all_gather x5 -> x0, waiting for transfers between devices: 303 us -> none  [the longest x1 63.3 us: expert_whole(): lax.all_gather(w_down, 'ctx', axis=2, tiled=True)]
    pallas_call x0 -> x1, Pallas kernels: none -> 135 us  [local_layer(): pl.pallas_call(layer, out_shape=(jax.ShapeDtypeStruct(queries.shape, BF16...]
    psum x1 -> x0, waiting for transfers between devices: 133 us -> none  [local(): proj = lax.psum(term.astype(jnp.bfloat16), 'exp').astype(jnp.float32)]
    reduce_scatter x1 -> x0, waiting for transfers between devices: 70.5 us -> none  [local(): lax.psum_scatter(contribution.astype(jnp.bfloat16), 'exp', scatter_dimens...]
    dot_general x9 -> x0, matrix products: 28 us -> none  [the longest x2 7.02 us: visit_half(): jnp.einsum('rhd,kd->hrk', query_half, keys_piece, preferred_element_type=...]
    le x2 -> x0, other arithmetic: 7.41 us -> none  [visit_half(): allowed = key_spots[None, None, :] <= spots[None, :, None]]
  transfers between devices with their start and end apart: 7 -> 0, of which waited for: 7 -> 0; matrix products, arithmetic and copies ran while one was open for 3% -> 0% of each run, Pallas kernels for 0% -> 0%
where the time goes in v1:
time: 138 us
  Pallas kernels  135 us (98%)
  local copies, waits for them, and re-layouts  2.23 us (2%)
    pallas_call x1, Pallas kernels, local_layer(): pl.pallas_call(layer, out_shape=(jax.ShapeDtypeStruct(queries.shape, BF16...  135 us

profile of v1, /device:TPU:6, one launch (start us, length us, event | category | flops | bytes accessed | tf_op | source)
XLA Modules:
  0.0 137.6 jit_solution(7187644681263186112)
XLA Ops:
  0.6 134.8 %layer.1 = (bf16[256,256]{1,0:T(8,128)(2,1)}, bf16[16,2048]{1,0:T(8,128)(2,1)}) custom-call(bf16[256,256]{1,0:T(8,128)(2,1)} %queries.1, bf16[256,512]{1,0:T(8,128)(2,1)} %keys.1, bf16[256,512]{1,0:T(8,128)(2,1)} %values.1, bf16[256,2048]{1,0:T(8,128)(2,1)} %out_proj.1, bf16[256,2048]{1,0:T(8,128)(2,1)} %resid.1, f32[1,2048]{1,0:T(1,128)} %bitcast.11, ...), custom_call_target="tpu_custom_call" | custom-call | tf_op jit(solution)/shard_map/layer/pallas_call | solution.py:396
  135.4 0.0 copy-start
  135.4 1.6 %copy.15 = bf16[256,256]{1,0:T(8,128)(2,1)} copy(bf16[256,256]{1,0:T(8,128)(2,1)} %get-tuple-element.4) | data formatting | bytes 262144
  137.0 0.0 copy-done
  137.0 0.6 copy.16
Async XLA Ops:
  135.4 1.6 %copy-start = (bf16[16,2048]{1,0:T(8,128)(2,1)S(1)}, bf16[16,2048]{1,0:T(8,128)(2,1)}, u32[]{:S(2)}) copy-start(bf16[16,2048]{1,0:T(8,128)(2,1)} %get-tuple-element.5) | copy-start | bytes 196612

commit v2 on v1

v2 whole, which is shorter than its diff:
```python
import math

import jax
import jax.numpy as jnp
from jax import lax
from jax.experimental import pallas as pl
from jax.experimental.pallas import tpu as pltpu
from jax.sharding import PartitionSpec as P

D = 2048
FF = 768
HEAD_SIZE = 128
KEY_HEAD_SHARERS = 4
SIDE = 4
RING = 16
TOKENS = 256
OWN = 16
HALF = D // 2
PART = OWN // 2
BLOCK = 2048
NEG = -1e30
F32 = jnp.float32
BF16 = jnp.bfloat16
MESH = pl.DeviceIdType.MESH


def wrap(index, size):
    return lax.rem(index + size, jnp.int32(size))


def remote(src, dst, sends, recvs, index, device):
    return pltpu.make_async_remote_copy(
        src_ref=src,
        dst_ref=dst,
        send_sem=sends.at[index],
        recv_sem=recvs.at[index],
        device_id=device,
        device_id_type=MESH,
    )


class TorusGather:
    def __init__(self, buf, sends, recvs, spot, devices, cut):
        first, second, core = spot
        to_first, to_second, to_core = devices
        up, down = wrap(first + 1, SIDE), wrap(first - 1, SIDE)
        above, below = wrap(second + 1, SIDE), wrap(second - 1, SIDE)
        across = wrap(second + 2, SIDE)
        size = buf.shape[3]
        own = buf.at[first, second, core]
        head = buf.at[down, second, core, pl.ds(0, cut)]
        tail = buf.at[up, second, core, pl.ds(cut, size - cut)]
        row = buf.at[:, second, core]
        row_head = buf.at[pl.ds(0, 2), below, core]
        row_tail = buf.at[pl.ds(2, 2), above, core]
        plan = [
            (own, to_first(up)),
            (own, to_first(down)),
            (head, to_first(up)),
            (tail, to_first(down)),
            (row, to_second(above)),
            (row, to_second(below)),
            (row_head, to_second(above)),
            (row_tail, to_second(below)),
            (row, to_core),
            (buf.at[:, below, core], to_core),
            (buf.at[:, above, core], to_core),
            (buf.at[:, across, core], to_core),
        ]
        self.copies = [
            remote(ref, ref, sends, recvs, index, device) for index, (ref, device) in enumerate(plan)
        ]

    def start(self, *which):
        for index in which:
            self.copies[index].start()

    def arrive(self, *which):
        for index in which:
            self.copies[index].wait_recv()

    def drain(self):
        for copy in self.copies:
            copy.wait_send()


class RingScatter:
    def __init__(self, terms, ring, sends, recvs, place):
        self.terms, self.ring, self.sends, self.recvs, self.place = terms, ring, sends, recvs, place

    def copy(self, way, far, step, src=None):
        dst = self.ring.at[way, far, step]
        sign = 1 - 2 * way
        device = {"exp": wrap(self.place + sign * (1 + far), RING)}
        return remote(dst if src is None else src, dst, self.sends, self.recvs, (way, far, step), device)

    def term(self, way, distance):
        return self.terms.at[wrap(self.place + (1 - 2 * way) * distance, RING)]

    def begin(self):
        self.copy(0, 1, 3, self.term(0, 8)).start()
        for step in (3, 2, 1, 0):
            for way in range(2):
                self.copy(way, 0, step, self.term(way, 2 * step + 1)).start()

    def arrived(self, way, step):
        self.copy(way, 0, step).wait_recv()
        total = self.ring[way, 0, step].astype(F32)
        if way == 0 or step < 3:
            self.copy(way, 1, step).wait_recv()
            total += self.ring[way, 1, step].astype(F32)
        return total

    def relay(self, step):
        for way in range(2):
            total = self.arrived(way, step) + self.term(way, 2 * step)[...].astype(F32)
            self.ring[way, 1, step] = total.astype(BF16)
            self.copy(way, 1, step - 1, self.ring.at[way, 1, step]).start()

    def total(self):
        return self.terms[self.place].astype(F32) + self.arrived(0, 0) + self.arrived(1, 0)

    def drain(self):
        for way in range(2):
            for step in range(4):
                self.copy(way, 0, step).wait_send()
                if way == 0 or step < 3:
                    self.copy(way, 1, step).wait_send()


class RingGather:
    def __init__(self, rows, sends, recvs, place):
        self.rows, self.sends, self.recvs, self.place = rows, sends, recvs, place

    def copy(self, way, far, step):
        sign = 1 - 2 * way
        ref = self.rows.at[wrap(self.place - sign * 2 * step, RING)]
        device = {"exp": wrap(self.place + sign * (1 + far), RING)}
        return remote(ref, ref, self.sends, self.recvs, (way, far, step), device)

    def send(self, step):
        for way in range(2):
            if way == 0 or step < 3:
                self.copy(way, 1, step).start()
        for way in range(2):
            self.copy(way, 0, step).start()

    def relay(self, step):
        for way in range(2):
            self.copy(way, 1, step - 1).wait_recv()
        self.send(step)

    def finish(self):
        for way in range(2):
            for step in range(4):
                self.copy(way, 0, step).wait_recv()
        self.copy(0, 1, 3).wait_recv()

    def drain(self):
        for way in range(2):
            for step in range(4):
                self.copy(way, 0, step).wait_send()
                if way == 0 or step < 3:
                    self.copy(way, 1, step).wait_send()


def pack(left, right):
    parts = [half.reshape(RING, PART, half.shape[1]) for half in (left, right)]
    return jnp.concatenate(parts, axis=1).astype(BF16)


def unpack(pieces):
    wide = pieces.astype(F32)
    width = wide.shape[2]
    return [wide[:, low : low + PART].reshape(RING * PART, width).astype(BF16) for low in (0, PART)]


def part_rows(rows, part):
    wide = rows.astype(F32).reshape(RING, OWN, rows.shape[1])
    return wide[:, part * PART : (part + 1) * PART].reshape(RING * PART, rows.shape[1])


def nt_dot(left, right):
    return lax.dot_general(left, right, (((1,), (1,)), ((), ())), preferred_element_type=F32)


def dot(left, right):
    return jnp.dot(left, right, preferred_element_type=F32)


def layer(
    queries, keys, values, out_proj, resid, gain, routes, gates, w_gate, w_up, w_down,
    attn_out, layer_out,
    kbuf, vbuf, abuf, bbuf, q_v, proj_v, resid_v, gain_v, routes_v, gates_v, weight_v, attn_v,
    terms, ring_one, normed, mixed, ring_two,
    loads, kv_sends, kv_recvs, w_sends, w_recvs, z_sends, z_recvs,
):
    ctx, place = lax.axis_index("ctx"), lax.axis_index("exp")
    x, y, core = lax.div(ctx, 8), lax.rem(lax.div(ctx, 2), 4), lax.rem(ctx, 2)

    def to_x(index):
        return {"ctx": index * 8 + y * 2 + core}

    def to_y(index):
        return {"ctx": x * 8 + index * 2 + core}

    to_core = {"ctx": x * 8 + y * 2 + (1 - core)}
    x_first = ((x, y, core), (to_x, to_y, to_core))
    y_first = ((y, x, core), (to_y, to_x, to_core))

    head_columns = pl.ds(pl.multiple_of(lax.div(place, KEY_HEAD_SHARERS) * HEAD_SIZE, HEAD_SIZE), HEAD_SIZE)
    own_rows = pl.ds(pl.multiple_of(place * OWN, OWN), OWN)
    own_a, own_b = abuf.at[x, y, core], bbuf.at[y, x, core]
    pairs = [
        (keys.at[:, head_columns], kbuf.at[x, y, core]),
        (values.at[:, head_columns], vbuf.at[y, x, core]),
        (queries, q_v),
        (w_gate, own_a.at[pl.ds(0, 64)]),
        (w_down.at[pl.ds(0, 32)], own_a.at[pl.ds(64, 32)]),
        (w_up, own_b.at[pl.ds(0, 64)]),
        (w_down.at[pl.ds(32, 32)], own_b.at[pl.ds(64, 32)]),
        (out_proj, proj_v),
        (resid.at[own_rows], resid_v),
        (gain, gain_v),
        (routes, routes_v),
        (gates, gates_v),
    ]
    local = [pltpu.make_async_copy(src, dst, loads.at[i]) for i, (src, dst) in enumerate(pairs)]
    for copy in local:
        copy.start()

    barrier = pltpu.get_barrier_semaphore()
    neighbours = [to_x(wrap(x + 1, SIDE)), to_x(wrap(x - 1, SIDE)), to_y(wrap(y + 1, SIDE)), to_y(wrap(y - 1, SIDE))]
    neighbours += [to_core] + [{"exp": wrap(place + far, RING)} for far in (1, -1, 2, -2)]
    for device in neighbours:
        pl.semaphore_signal(barrier, inc=1, device_id=device, device_id_type=MESH)
    pl.semaphore_wait(barrier, len(neighbours))

    k_gather = TorusGather(kbuf, kv_sends.at[0], kv_recvs.at[0], *x_first, 128)
    v_gather = TorusGather(vbuf, kv_sends.at[1], kv_recvs.at[1], *y_first, 128)
    a_gather = TorusGather(abuf, w_sends.at[0], w_recvs.at[0], *x_first, 48)
    b_gather = TorusGather(bbuf, w_sends.at[1], w_recvs.at[1], *y_first, 48)
    heads, experts = (k_gather, v_gather), (a_gather, b_gather)

    for index, gather in enumerate(heads):
        local[index].wait()
        gather.start(0, 1)
    for gather in heads:
        gather.arrive(0)
        gather.start(2)
        gather.arrive(1)
        gather.start(3)
    for gather in heads:
        gather.arrive(2, 3)
        gather.start(4, 5, 8)
    for copy in local[2:]:
        copy.wait()
    for gather in experts:
        gather.start(0, 1)
    for gather in heads:
        gather.arrive(4)
        gather.start(6, 9)
        gather.arrive(5)
        gather.start(7, 10)

    all_gates = gates_v[...]
    share = all_gates / jnp.sum(all_gates, axis=0, keepdims=True)
    here = jnp.sum(jnp.where(routes_v[...] == place, share, 0.0), axis=0, keepdims=True)
    weight_v[...] = jnp.broadcast_to(here, (128, TOKENS)).T

    for gather in heads:
        gather.arrive(6, 7)
        gather.start(11)
    for gather in experts:
        gather.arrive(0)
        gather.start(2)
        gather.arrive(1)
        gather.start(3)
    for gather in heads:
        gather.arrive(8, 9, 10, 11)

    scale = math.log2(math.e) / math.sqrt(HEAD_SIZE)
    offset = lax.rem(ctx, 8) * TOKENS
    half_rows = RING * PART

    def query_of(part):
        rows = part_rows(q_v[...], part)
        return jnp.concatenate([rows[:, :HEAD_SIZE], rows[:, HEAD_SIZE:]], axis=0).astype(BF16)

    def visit(query, part, index, state, masked=False):
        peak, mass, accum = state
        some_keys = kbuf[index].reshape(BLOCK, HEAD_SIZE)
        some_values = vbuf[:, index].reshape(BLOCK, HEAD_SIZE)
        scores = nt_dot(query, some_keys)
        if masked:
            row = lax.broadcasted_iota(jnp.int32, (2 * half_rows, 1), 0) & (half_rows - 1)
            token = (row >> 3) * OWN + (row & (PART - 1)) + part * PART + offset
            column = lax.broadcasted_iota(jnp.int32, scores.shape, 1)
            scores = jnp.where(column <= token, scores, NEG)
        new_peak = jnp.maximum(peak, jnp.max(scores, axis=1, keepdims=True))
        weights = jnp.exp2((scores - new_peak) * scale)
        fade = jnp.exp2((peak - new_peak) * scale)
        some = weights[:, :128]
        for low in range(128, BLOCK, 128):
            some = some + weights[:, low : low + 128]
        mass = mass * fade + some
        accum = accum * fade + dot(weights.astype(BF16), some_values)
        return (new_peak, mass, accum)

    middle = lax.div(x + 1, 2)

    def first_blocks(part):
        state = (
            jnp.full((2 * half_rows, 1), NEG, F32),
            jnp.zeros((2 * half_rows, 128), F32),
            jnp.zeros((2 * half_rows, HEAD_SIZE), F32),
        )
        return lax.fori_loop(0, middle, lambda index, state: visit(query_of(part), part, index, state), state)

    def last_blocks(part, state):
        state = lax.fori_loop(middle, x, lambda index, state: visit(query_of(part), part, index, state), state)
        _, mass, accum = visit(query_of(part), part, x, state, masked=True)
        result = accum / jnp.sum(mass, axis=1, keepdims=True)
        return jnp.concatenate([result[:half_rows], result[half_rows:]], axis=1)

    def project(part, rows):
        halves = [dot(rows.astype(BF16), proj_v[:, low : low + HALF]) for low in (0, HALF)]
        terms[part] = pack(*halves)

    def norm(part):
        total = scatter_one[part].total()
        rows = resid_v[...].astype(F32)[part * PART : (part + 1) * PART]
        hidden = rows + jnp.concatenate([total[:PART], total[PART:]], axis=1)
        spread = lax.rsqrt(jnp.mean(hidden * hidden, axis=1, keepdims=True) + 1e-06)
        own = hidden * spread * gain_v[...]
        normed[part, place] = jnp.concatenate([own[:, :HALF], own[:, HALF:]], axis=0).astype(BF16)
        return hidden

    def expert(part):
        left, right = unpack(normed[part])
        gate_sum = dot(left, abuf[:2, :, :, :64].reshape(HALF, FF))
        gate_sum += dot(right, abuf[2:, :, :, :64].reshape(HALF, FF))
        up_sum = jnp.zeros(gate_sum.shape, F32)
        for quarter in range(SIDE):
            low = quarter % 2 * 512
            some = (left, right)[quarter // 2][:, low : low + 512]
            up_sum += dot(some, bbuf[:, quarter, :, :64].reshape(512, FF))
        act = (gate_sum / (1.0 + jnp.exp(-gate_sum)) * up_sum).astype(BF16)
        weight = part_rows(weight_v[...], part)[:, :1]

        def down(quarter):
            rows = jnp.concatenate([abuf[quarter, :, :, 64:], bbuf[:, quarter, :, 64:]], axis=2)
            some = nt_dot(act, rows.reshape(512, FF)).astype(BF16).astype(F32)
            return jnp.where(weight > 0.0, weight * some, 0.0)

        for low in range(2):
            mixed[part, :, :, low * 512 : low * 512 + 512] = pack(down(low), down(low + 2))

    scatter_one = [RingScatter(terms.at[i], ring_one.at[i], z_sends.at[i], z_recvs.at[i], place) for i in range(2)]
    spread_rows = [RingGather(normed.at[i], z_sends.at[2 + i], z_recvs.at[2 + i], place) for i in range(2)]
    scatter_two = [
        RingScatter(mixed.at[i], ring_two.at[i], z_sends.at[4 + i], z_recvs.at[4 + i], place) for i in range(2)
    ]

    state = first_blocks(0)
    for gather in experts:
        gather.arrive(2, 3)
        gather.start(4, 5, 8)
    early = last_blocks(0, state)
    project(0, early)
    scatter_one[0].begin()
    state = first_blocks(1)
    scatter_one[0].relay(3)
    late = last_blocks(1, state)
    scatter_one[0].relay(2)
    project(1, late)
    scatter_one[1].begin()
    pair = [rows.reshape(RING, PART, 2 * HEAD_SIZE) for rows in (early, late)]
    attn_v[...] = jnp.concatenate(pair, axis=1).reshape(TOKENS, 2 * HEAD_SIZE).astype(BF16)
    attn_copy = pltpu.make_async_copy(attn_v, attn_out, loads.at[len(pairs)])
    attn_copy.start()
    scatter_one[0].relay(1)
    for gather in experts:
        gather.arrive(4)
        gather.start(6, 9)
        gather.arrive(5)
        gather.start(7, 10)
    scatter_one[1].relay(3)
    hidden_early = norm(0)
    spread_rows[0].send(0)
    scatter_one[1].relay(2)
    spread_rows[0].relay(1)
    scatter_one[1].relay(1)
    for gather in experts:
        gather.arrive(6, 7)
        gather.start(11)
    spread_rows[0].relay(2)
    hidden_late = norm(1)
    spread_rows[1].send(0)
    spread_rows[0].relay(3)
    spread_rows[1].relay(1)
    for gather in experts:
        gather.arrive(8, 9, 10, 11)
    spread_rows[0].finish()
    expert(0)
    scatter_two[0].begin()
    spread_rows[1].relay(2)
    scatter_two[0].relay(3)
    spread_rows[1].relay(3)
    scatter_two[0].relay(2)
    spread_rows[1].finish()
    expert(1)
    scatter_two[1].begin()
    scatter_two[0].relay(1)
    scatter_two[1].relay(3)
    done = []
    for part, hidden in enumerate((hidden_early, hidden_late)):
        total = scatter_two[part].total()
        done.append(hidden + jnp.concatenate([total[:PART], total[PART:]], axis=1))
        if part == 0:
            scatter_two[1].relay(2)
            scatter_two[1].relay(1)
    layer_out[...] = jnp.concatenate(done, axis=0).astype(BF16)

    attn_copy.wait()
    for gather in (*heads, *experts, *scatter_one, *spread_rows, *scatter_two):
        gather.drain()


def local_layer(queries, keys, values, out_proj, resid, norm_gain, routes, gates, w_gate, w_up, w_down):
    anywhere = pl.BlockSpec(memory_space=pl.ANY)
    torus = (SIDE, SIDE, 2)
    pieces = (2, RING, 2 * PART, HALF)
    ring = (2, 2, 2, 4, 2 * PART, HALF)
    ring_sems = pltpu.SemaphoreType.DMA((6, 2, 2, 4))
    gather_sems = pltpu.SemaphoreType.DMA((2, 12))
    return pl.pallas_call(
        layer,
        out_shape=(
            jax.ShapeDtypeStruct(queries.shape, BF16),
            jax.ShapeDtypeStruct((OWN, D), BF16),
        ),
        in_specs=[anywhere] * 11,
        out_specs=(anywhere, pl.BlockSpec(memory_space=pltpu.VMEM)),
        scratch_shapes=[
            pltpu.VMEM((*torus, TOKENS, HEAD_SIZE), BF16),
            pltpu.VMEM((*torus, TOKENS, HEAD_SIZE), BF16),
            pltpu.VMEM((*torus, 96, FF), BF16),
            pltpu.VMEM((*torus, 96, FF), BF16),
            pltpu.VMEM(queries.shape, BF16),
            pltpu.VMEM(out_proj.shape, BF16),
            pltpu.VMEM((OWN, D), BF16),
            pltpu.VMEM((1, D), F32),
            pltpu.VMEM((8, TOKENS), jnp.int32),
            pltpu.VMEM((8, TOKENS), F32),
            pltpu.VMEM((TOKENS, 128), F32),
            pltpu.VMEM(queries.shape, BF16),
            pltpu.VMEM(pieces, BF16),
            pltpu.VMEM(ring, BF16),
            pltpu.VMEM(pieces, BF16),
            pltpu.VMEM(pieces, BF16),
            pltpu.VMEM(ring, BF16),
            pltpu.SemaphoreType.DMA((13,)),
            gather_sems,
            gather_sems,
            gather_sems,
            gather_sems,
            ring_sems,
            ring_sems,
        ],
        compiler_params=pltpu.CompilerParams(
            collective_id=0, has_side_effects=True, vmem_limit_bytes=56 * 1024 * 1024
        ),
        name="layer",
    )(
        queries,
        keys,
        values,
        out_proj,
        resid,
        norm_gain.reshape(1, D),
        routes.T,
        gates.T,
        w_gate[0],
        w_up[0],
        w_down[0].T,
    )


def solution(mesh):
    placed = (
        P("ctx", "exp"),
        P("ctx", None),
        P("ctx", None),
        P("exp", None),
        P("ctx", None),
        P(),
        P("ctx", None),
        P("ctx", None),
        P("exp", "ctx", None),
        P("exp", "ctx", None),
        P("exp", None, "ctx"),
    )
    return jax.shard_map(
        local_layer,
        mesh=mesh,
        in_specs=placed,
        out_specs=(P("ctx", "exp"), P(("ctx", "exp"), None)),
        check_vma=False,
    )
```

time: 138 us -> 115 us (0.83)
  Pallas kernels: 135 us -> 112 us
    pallas_call x1, Pallas kernels: 135 us -> 112 us  [local_layer(): pl.pallas_call(layer, out_shape=(jax.ShapeDtypeStruct(queries.shape, BF16...]
where the time goes in v2:
time: 115 us
  Pallas kernels  112 us (97%)
  local copies, waits for them, and re-layouts  2.23 us (2%)
    pallas_call x1, Pallas kernels, local_layer(): pl.pallas_call(layer, out_shape=(jax.ShapeDtypeStruct(queries.shape, BF16...  112 us

profile of v2, /device:TPU:6, one launch (start us, length us, event | category | flops | bytes accessed | tf_op | source)
XLA Modules:
  0.0 115.1 jit_solution(3509154312688841209)
XLA Ops:
  0.6 112.2 %layer.1 = (bf16[256,256]{1,0:T(8,128)(2,1)}, bf16[16,2048]{1,0:T(8,128)(2,1)}) custom-call(bf16[256,256]{1,0:T(8,128)(2,1)} %queries.1, bf16[256,512]{1,0:T(8,128)(2,1)} %keys.1, bf16[256,512]{1,0:T(8,128)(2,1)} %values.1, bf16[256,2048]{1,0:T(8,128)(2,1)} %out_proj.1, bf16[256,2048]{1,0:T(8,128)(2,1)} %resid.1, f32[1,2048]{1,0:T(1,128)} %bitcast.11, ...), custom_call_target="tpu_custom_call" | custom-call | tf_op jit(solution)/shard_map/layer/pallas_call | solution.py:437
  112.9 0.0 copy-start
  112.9 1.6 %copy.15 = bf16[256,256]{1,0:T(8,128)(2,1)} copy(bf16[256,256]{1,0:T(8,128)(2,1)} %get-tuple-element.4) | data formatting | bytes 262144
  114.5 0.0 copy-done
  114.5 0.6 copy.16
Async XLA Ops:
  112.9 1.6 %copy-start = (bf16[16,2048]{1,0:T(8,128)(2,1)S(1)}, bf16[16,2048]{1,0:T(8,128)(2,1)}, u32[]{:S(2)}) copy-start(bf16[16,2048]{1,0:T(8,128)(2,1)} %get-tuple-element.5) | copy-start | bytes 196612

commit v3 on v2

--- a/solution.py
+++ b/solution.py
@@ -40,33 +40,21 @@
 
 
 class TorusGather:
-    def __init__(self, buf, sends, recvs, spot, devices, cut):
+    def __init__(self, buf, sends, recvs, spot, devices):
         first, second, core = spot
         to_first, to_second, to_core = devices
-        up, down = wrap(first + 1, SIDE), wrap(first - 1, SIDE)
         above, below = wrap(second + 1, SIDE), wrap(second - 1, SIDE)
-        across = wrap(second + 2, SIDE)
-        size = buf.shape[3]
+        self.rows = (second, below, above, wrap(second + 2, SIDE))
         own = buf.at[first, second, core]
-        head = buf.at[down, second, core, pl.ds(0, cut)]
-        tail = buf.at[up, second, core, pl.ds(cut, size - cut)]
         row = buf.at[:, second, core]
-        row_head = buf.at[pl.ds(0, 2), below, core]
-        row_tail = buf.at[pl.ds(2, 2), above, core]
-        plan = [
-            (own, to_first(up)),
-            (own, to_first(down)),
-            (head, to_first(up)),
-            (tail, to_first(down)),
+        plan = [(own, to_first(wrap(first + far, SIDE))) for far in (1, -1, 2)]
+        plan += [
             (row, to_second(above)),
             (row, to_second(below)),
-            (row_head, to_second(above)),
-            (row_tail, to_second(below)),
-            (row, to_core),
-            (buf.at[:, below, core], to_core),
-            (buf.at[:, above, core], to_core),
-            (buf.at[:, across, core], to_core),
+            (buf.at[pl.ds(0, 2), below, core], to_second(above)),
+            (buf.at[pl.ds(2, 2), above, core], to_second(below)),
         ]
+        plan += [(buf.at[:, other, core], to_core) for other in self.rows]
         self.copies = [
             remote(ref, ref, sends, recvs, index, device) for index, (ref, device) in enumerate(plan)
         ]
@@ -191,7 +179,7 @@
 def layer(
     queries, keys, values, out_proj, resid, gain, routes, gates, w_gate, w_up, w_down,
     attn_out, layer_out,
-    kbuf, vbuf, abuf, bbuf, q_v, proj_v, resid_v, gain_v, routes_v, gates_v, weight_v, attn_v,
+    heads_x, heads_y, abuf, bbuf, q_v, proj_v, resid_v, gain_v, routes_v, gates_v, weight_v, attn_v,
     terms, ring_one, normed, mixed, ring_two,
     loads, kv_sends, kv_recvs, w_sends, w_recvs, z_sends, z_recvs,
 ):
@@ -211,9 +199,12 @@
     head_columns = pl.ds(pl.multiple_of(lax.div(place, KEY_HEAD_SHARERS) * HEAD_SIZE, HEAD_SIZE), HEAD_SIZE)
     own_rows = pl.ds(pl.multiple_of(place * OWN, OWN), OWN)
     own_a, own_b = abuf.at[x, y, core], bbuf.at[y, x, core]
+    half_rows = RING * PART
     pairs = [
-        (keys.at[:, head_columns], kbuf.at[x, y, core]),
-        (values.at[:, head_columns], vbuf.at[y, x, core]),
+        (keys.at[pl.ds(0, half_rows), head_columns], heads_x.at[x, y, core, 0]),
+        (values.at[pl.ds(0, half_rows), head_columns], heads_x.at[x, y, core, 1]),
+        (keys.at[pl.ds(half_rows, half_rows), head_columns], heads_y.at[y, x, core, 0]),
+        (values.at[pl.ds(half_rows, half_rows), head_columns], heads_y.at[y, x, core, 1]),
         (queries, q_v),
         (w_gate, own_a.at[pl.ds(0, 64)]),
         (w_down.at[pl.ds(0, 32)], own_a.at[pl.ds(64, 32)]),
@@ -230,73 +221,63 @@
         copy.start()
 
     barrier = pltpu.get_barrier_semaphore()
-    neighbours = [to_x(wrap(x + 1, SIDE)), to_x(wrap(x - 1, SIDE)), to_y(wrap(y + 1, SIDE)), to_y(wrap(y - 1, SIDE))]
-    neighbours += [to_core] + [{"exp": wrap(place + far, RING)} for far in (1, -1, 2, -2)]
+    neighbours = [to_core] + [{"exp": wrap(place + far, RING)} for far in (1, -1, 2, -2)]
+    for far in (1, -1, 2):
+        neighbours += [to_x(wrap(x + far, SIDE)), to_y(wrap(y + far, SIDE))]
     for device in neighbours:
         pl.semaphore_signal(barrier, inc=1, device_id=device, device_id_type=MESH)
     pl.semaphore_wait(barrier, len(neighbours))
 
-    k_gather = TorusGather(kbuf, kv_sends.at[0], kv_recvs.at[0], *x_first, 128)
-    v_gather = TorusGather(vbuf, kv_sends.at[1], kv_recvs.at[1], *y_first, 128)
-    a_gather = TorusGather(abuf, w_sends.at[0], w_recvs.at[0], *x_first, 48)
-    b_gather = TorusGather(bbuf, w_sends.at[1], w_recvs.at[1], *y_first, 48)
-    heads, experts = (k_gather, v_gather), (a_gather, b_gather)
+    x_heads = TorusGather(heads_x, kv_sends.at[0], kv_recvs.at[0], *x_first)
+    y_heads = TorusGather(heads_y, kv_sends.at[1], kv_recvs.at[1], *y_first)
+    a_gather = TorusGather(abuf, w_sends.at[0], w_recvs.at[0], *x_first)
+    b_gather = TorusGather(bbuf, w_sends.at[1], w_recvs.at[1], *y_first)
+    heads, experts = (x_heads, y_heads), (a_gather, b_gather)
 
     for index, gather in enumerate(heads):
-        local[index].wait()
-        gather.start(0, 1)
-    for gather in heads:
-        gather.arrive(0)
-        gather.start(2)
-        gather.arrive(1)
-        gather.start(3)
-    for gather in heads:
-        gather.arrive(2, 3)
-        gather.start(4, 5, 8)
-    for copy in local[2:]:
+        local[2 * index].wait()
+        local[2 * index + 1].wait()
+        gather.start(0, 1, 2)
+    for copy in local[4:]:
         copy.wait()
-    for gather in experts:
-        gather.start(0, 1)
-    for gather in heads:
-        gather.arrive(4)
-        gather.start(6, 9)
-        gather.arrive(5)
-        gather.start(7, 10)
 
     all_gates = gates_v[...]
     share = all_gates / jnp.sum(all_gates, axis=0, keepdims=True)
     here = jnp.sum(jnp.where(routes_v[...] == place, share, 0.0), axis=0, keepdims=True)
     weight_v[...] = jnp.broadcast_to(here, (128, TOKENS)).T
 
-    for gather in heads:
-        gather.arrive(6, 7)
-        gather.start(11)
-    for gather in experts:
-        gather.arrive(0)
-        gather.start(2)
-        gather.arrive(1)
-        gather.start(3)
-    for gather in heads:
-        gather.arrive(8, 9, 10, 11)
-
     scale = math.log2(math.e) / math.sqrt(HEAD_SIZE)
-    offset = lax.rem(ctx, 8) * TOKENS
-    half_rows = RING * PART
+    key = lax.broadcasted_iota(jnp.int32, (1, BLOCK // 2), 1)
+    in_chip = ((key >> 7) & 1) * TOKENS + (key & 127)
 
     def query_of(part):
         rows = part_rows(q_v[...], part)
         return jnp.concatenate([rows[:, :HEAD_SIZE], rows[:, HEAD_SIZE:]], axis=0).astype(BF16)
 
-    def visit(query, part, index, state, masked=False):
-        peak, mass, accum = state
-        some_keys = kbuf[index].reshape(BLOCK, HEAD_SIZE)
-        some_values = vbuf[:, index].reshape(BLOCK, HEAD_SIZE)
-        scores = nt_dot(query, some_keys)
-        if masked:
-            row = lax.broadcasted_iota(jnp.int32, (2 * half_rows, 1), 0) & (half_rows - 1)
-            token = (row >> 3) * OWN + (row & (PART - 1)) + part * PART + offset
-            column = lax.broadcasted_iota(jnp.int32, scores.shape, 1)
-            scores = jnp.where(column <= token, scores, NEG)
+    def start_of(part):
+        state = (
+            jnp.full((2 * half_rows, 1), NEG, F32),
+            jnp.zeros((2 * half_rows, 128), F32),
+            jnp.zeros((2 * half_rows, HEAD_SIZE), F32),
+        )
+        return (part, query_of(part), state)
+
+    def visit(task, index):
+        part, query, (peak, mass, accum) = task
+        at_y, at_x = x_heads.rows[index], y_heads.rows[index]
+
+        def both(kind):
+            pieces = (heads_x[:, at_y, :, kind], heads_y[:, at_x, :, kind])
+            return jnp.concatenate([piece.reshape(BLOCK // 2, HEAD_SIZE) for piece in pieces], axis=0)
+
+        scores = nt_dot(query, both(0))
+        spots = (
+            (key >> 8) * (8 * TOKENS) + at_y * (2 * TOKENS) + in_chip,
+            (key >> 8) * (2 * TOKENS) + at_x * (8 * TOKENS) + in_chip + half_rows,
+        )
+        row = lax.broadcasted_iota(jnp.int32, (2 * half_rows, 1), 0) & (half_rows - 1)
+        token = (row >> 3) * OWN + (row & (PART - 1)) + part * PART + ctx * TOKENS
+        scores = jnp.where(jnp.concatenate(spots, axis=1) <= token, scores, NEG)
         new_peak = jnp.maximum(peak, jnp.max(scores, axis=1, keepdims=True))
         weights = jnp.exp2((scores - new_peak) * scale)
         fade = jnp.exp2((peak - new_peak) * scale)
@@ -304,22 +285,11 @@
         for low in range(128, BLOCK, 128):
             some = some + weights[:, low : low + 128]
         mass = mass * fade + some
-        accum = accum * fade + dot(weights.astype(BF16), some_values)
-        return (new_peak, mass, accum)
-
-    middle = lax.div(x + 1, 2)
-
-    def first_blocks(part):
-        state = (
-            jnp.full((2 * half_rows, 1), NEG, F32),
-            jnp.zeros((2 * half_rows, 128), F32),
-            jnp.zeros((2 * half_rows, HEAD_SIZE), F32),
-        )
-        return lax.fori_loop(0, middle, lambda index, state: visit(query_of(part), part, index, state), state)
-
-    def last_blocks(part, state):
-        state = lax.fori_loop(middle, x, lambda index, state: visit(query_of(part), part, index, state), state)
-        _, mass, accum = visit(query_of(part), part, x, state, masked=True)
+        accum = accum * fade + dot(weights.astype(BF16), both(1))
+        return (part, query, (new_peak, mass, accum))
+
+    def end_of(task):
+        _, _, (_, mass, accum) = task
         result = accum / jnp.sum(mass, axis=1, keepdims=True)
         return jnp.concatenate([result[:half_rows], result[half_rows:]], axis=1)
 
@@ -362,69 +332,90 @@
         RingScatter(mixed.at[i], ring_two.at[i], z_sends.at[4 + i], z_recvs.at[4 + i], place) for i in range(2)
     ]
 
-    state = first_blocks(0)
+    early, late = start_of(0), start_of(1)
+    for gather in heads:
+        gather.arrive(0, 1, 2)
+        gather.start(3, 4, 7)
+    for gather in heads:
+        gather.arrive(7)
+    early = visit(early, 0)
+    late = visit(late, 0)
+    for gather in heads:
+        gather.arrive(3)
+        gather.start(5, 8)
+        gather.arrive(4)
+        gather.start(6, 9)
+    for gather in heads:
+        gather.arrive(8)
+    early = visit(early, 1)
+    for gather in heads:
+        gather.arrive(9)
+    early = visit(early, 2)
+    for gather in heads:
+        gather.arrive(5, 6)
+        gather.start(10)
     for gather in experts:
-        gather.arrive(2, 3)
-        gather.start(4, 5, 8)
-    early = last_blocks(0, state)
+        gather.start(0, 1, 2)
+    for gather in heads:
+        gather.arrive(10)
+    early = end_of(visit(early, 3))
     project(0, early)
     scatter_one[0].begin()
-    state = first_blocks(1)
-    scatter_one[0].relay(3)
-    late = last_blocks(1, state)
-    scatter_one[0].relay(2)
+    late = visit(late, 1)
+    late = visit(late, 2)
+    late = end_of(visit(late, 3))
     project(1, late)
     scatter_one[1].begin()
     pair = [rows.reshape(RING, PART, 2 * HEAD_SIZE) for rows in (early, late)]
     attn_v[...] = jnp.concatenate(pair, axis=1).reshape(TOKENS, 2 * HEAD_SIZE).astype(BF16)
     attn_copy = pltpu.make_async_copy(attn_v, attn_out, loads.at[len(pairs)])
     attn_copy.start()
-    scatter_one[0].relay(1)
+    scatter_one[0].relay(3)
     for gather in experts:
+        gather.arrive(0, 1, 2)
+        gather.start(3, 4, 7)
+    scatter_one[1].relay(3)
+    for step in (2, 1):
+        for part in range(2):
+            scatter_one[part].relay(step)
+    hidden = []
+    for part in range(2):
+        hidden.append(norm(part))
+        spread_rows[part].send(0)
+    for gather in experts:
+        gather.arrive(3)
+        gather.start(5, 8)
         gather.arrive(4)
         gather.start(6, 9)
-        gather.arrive(5)
-        gather.start(7, 10)
-    scatter_one[1].relay(3)
-    hidden_early = norm(0)
-    spread_rows[0].send(0)
-    scatter_one[1].relay(2)
-    spread_rows[0].relay(1)
-    scatter_one[1].relay(1)
+    for step in (1, 2, 3):
+        for part in range(2):
+            spread_rows[part].relay(step)
+        if step == 2:
+            for gather in experts:
+                gather.arrive(5, 6)
+                gather.start(10)
     for gather in experts:
-        gather.arrive(6, 7)
-        gather.start(11)
-    spread_rows[0].relay(2)
-    hidden_late = norm(1)
-    spread_rows[1].send(0)
-    spread_rows[0].relay(3)
-    spread_rows[1].relay(1)
-    for gather in experts:
-        gather.arrive(8, 9, 10, 11)
-    spread_rows[0].finish()
-    expert(0)
-    scatter_two[0].begin()
-    spread_rows[1].relay(2)
-    scatter_two[0].relay(3)
-    spread_rows[1].relay(3)
-    scatter_two[0].relay(2)
-    spread_rows[1].finish()
-    expert(1)
-    scatter_two[1].begin()
-    scatter_two[0].relay(1)
-    scatter_two[1].relay(3)
+        gather.arrive(7, 8, 9, 10)
+    for part in range(2):
+        spread_rows[part].finish()
+        expert(part)
+        scatter_two[part].begin()
+    attn_copy.wait()
+    for gather in (*heads, *experts):
+        gather.drain()
+    for step in (3, 2, 1):
+        for part in range(2):
+            scatter_two[part].relay(step)
+        if step > 1:
+            (scatter_one, spread_rows)[step - 2][0].drain()
+            (scatter_one, spread_rows)[step - 2][1].drain()
     done = []
-    for part, hidden in enumerate((hidden_early, hidden_late)):
+    for part in range(2):
         total = scatter_two[part].total()
-        done.append(hidden + jnp.concatenate([total[:PART], total[PART:]], axis=1))
-        if part == 0:
-            scatter_two[1].relay(2)
-            scatter_two[1].relay(1)
+        done.append(hidden[part] + jnp.concatenate([total[:PART], total[PART:]], axis=1))
     layer_out[...] = jnp.concatenate(done, axis=0).astype(BF16)
-
-    attn_copy.wait()
-    for gather in (*heads, *experts, *scatter_one, *spread_rows, *scatter_two):
-        gather.drain()
+    for part in range(2):
+        scatter_two[part].drain()
 
 
 def local_layer(queries, keys, values, out_proj, resid, norm_gain, routes, gates, w_gate, w_up, w_down):
@@ -433,7 +424,7 @@
     pieces = (2, RING, 2 * PART, HALF)
     ring = (2, 2, 2, 4, 2 * PART, HALF)
     ring_sems = pltpu.SemaphoreType.DMA((6, 2, 2, 4))
-    gather_sems = pltpu.SemaphoreType.DMA((2, 12))
+    gather_sems = pltpu.SemaphoreType.DMA((2, 11))
     return pl.pallas_call(
         layer,
         out_shape=(
@@ -443,8 +434,8 @@
         in_specs=[anywhere] * 11,
         out_specs=(anywhere, pl.BlockSpec(memory_space=pltpu.VMEM)),
         scratch_shapes=[
-            pltpu.VMEM((*torus, TOKENS, HEAD_SIZE), BF16),
-            pltpu.VMEM((*torus, TOKENS, HEAD_SIZE), BF16),
+            pltpu.VMEM((*torus, 2, TOKENS // 2, HEAD_SIZE), BF16),
+            pltpu.VMEM((*torus, 2, TOKENS // 2, HEAD_SIZE), BF16),
             pltpu.VMEM((*torus, 96, FF), BF16),
             pltpu.VMEM((*torus, 96, FF), BF16),
             pltpu.VMEM(queries.shape, BF16),
@@ -460,7 +451,7 @@
             pltpu.VMEM(pieces, BF16),
             pltpu.VMEM(pieces, BF16),
             pltpu.VMEM(ring, BF16),
-            pltpu.SemaphoreType.DMA((13,)),
+            pltpu.SemaphoreType.DMA((15,)),
             gather_sems,
             gather_sems,
             gather_sems,

time: 115 us -> 103 us (0.90); the launches traced: 115 us -> 102 us
  Pallas kernels: 112 us -> 98.6 us
    pallas_call x1, Pallas kernels: 112 us -> 98.6 us  [local_layer(): pl.pallas_call(layer, out_shape=(jax.ShapeDtypeStruct(queries.shape, BF16...]
where the time goes in v3:
time: 103 us; the launch traced here: 102 us
  Pallas kernels  98.6 us (96%)
  local copies, waits for them, and re-layouts  2.23 us (2%)
    pallas_call x1, Pallas kernels, local_layer(): pl.pallas_call(layer, out_shape=(jax.ShapeDtypeStruct(queries.shape, BF16...  98.6 us
    unnamed x4, local copies, waits for them, and re-layouts  2.23 us

profile of v3, /device:TPU:6, one launch (start us, length us, event | category | flops | bytes accessed | tf_op | source)
XLA Modules:
  0.0 101.5 jit_solution(6472903864006144158)
XLA Ops:
  0.6 98.6 %layer.1 = (bf16[256,256]{1,0:T(8,128)(2,1)}, bf16[16,2048]{1,0:T(8,128)(2,1)}) custom-call(bf16[256,256]{1,0:T(8,128)(2,1)} %queries.1, bf16[256,512]{1,0:T(8,128)(2,1)} %keys.1, bf16[256,512]{1,0:T(8,128)(2,1)} %values.1, bf16[256,2048]{1,0:T(8,128)(2,1)} %out_proj.1, bf16[256,2048]{1,0:T(8,128)(2,1)} %resid.1, f32[1,2048]{1,0:T(1,128)} %bitcast.11, ...), custom_call_target="tpu_custom_call" | custom-call | tf_op jit(solution)/shard_map/layer/pallas_call | solution.py:428
  99.3 0.0 copy-start
  99.3 1.6 %copy.15 = bf16[256,256]{1,0:T(8,128)(2,1)} copy(bf16[256,256]{1,0:T(8,128)(2,1)} %get-tuple-element.4) | data formatting | bytes 262144
  100.9 0.0 copy-done
  100.9 0.6 copy.16
Async XLA Ops:
  99.3 1.6 %copy-start = (bf16[16,2048]{1,0:T(8,128)(2,1)S(1)}, bf16[16,2048]{1,0:T(8,128)(2,1)}, u32[]{:S(2)}) copy-start(bf16[16,2048]{1,0:T(8,128)(2,1)} %get-tuple-element.5) | copy-start | bytes 196612

commit v4 on v3

--- a/solution.py
+++ b/solution.py
@@ -73,23 +73,25 @@
 
 
 class RingScatter:
-    def __init__(self, terms, ring, sends, recvs, place):
+    def __init__(self, terms, ring, sends, recvs, place, sign):
         self.terms, self.ring, self.sends, self.recvs, self.place = terms, ring, sends, recvs, place
+        self.signs = (sign, -sign)
 
     def copy(self, way, far, step, src=None):
         dst = self.ring.at[way, far, step]
-        sign = 1 - 2 * way
-        device = {"exp": wrap(self.place + sign * (1 + far), RING)}
+        device = {"exp": wrap(self.place + self.signs[way] * (1 + far), RING)}
         return remote(dst if src is None else src, dst, self.sends, self.recvs, (way, far, step), device)
 
     def term(self, way, distance):
-        return self.terms.at[wrap(self.place + (1 - 2 * way) * distance, RING)]
+        return self.terms.at[wrap(self.place + self.signs[way] * distance, RING)]
+
+    def lend(self, step):
+        for way in range(2):
+            self.copy(way, 0, step, self.term(way, 2 * step + 1)).start()
 
     def begin(self):
         self.copy(0, 1, 3, self.term(0, 8)).start()
-        for step in (3, 2, 1, 0):
-            for way in range(2):
-                self.copy(way, 0, step, self.term(way, 2 * step + 1)).start()
+        self.lend(3)
 
     def arrived(self, way, step):
         self.copy(way, 0, step).wait_recv()
@@ -104,6 +106,7 @@
             total = self.arrived(way, step) + self.term(way, 2 * step)[...].astype(F32)
             self.ring[way, 1, step] = total.astype(BF16)
             self.copy(way, 1, step - 1, self.ring.at[way, 1, step]).start()
+        self.lend(step - 1)
 
     def total(self):
         return self.terms[self.place].astype(F32) + self.arrived(0, 0) + self.arrived(1, 0)
@@ -117,11 +120,12 @@
 
 
 class RingGather:
-    def __init__(self, rows, sends, recvs, place):
+    def __init__(self, rows, sends, recvs, place, sign):
         self.rows, self.sends, self.recvs, self.place = rows, sends, recvs, place
+        self.signs = (sign, -sign)
 
     def copy(self, way, far, step):
-        sign = 1 - 2 * way
+        sign = self.signs[way]
         ref = self.rows.at[wrap(self.place - sign * 2 * step, RING)]
         device = {"exp": wrap(self.place + sign * (1 + far), RING)}
         return remote(ref, ref, self.sends, self.recvs, (way, far, step), device)
@@ -326,11 +330,10 @@
         for low in range(2):
             mixed[part, :, :, low * 512 : low * 512 + 512] = pack(down(low), down(low + 2))
 
-    scatter_one = [RingScatter(terms.at[i], ring_one.at[i], z_sends.at[i], z_recvs.at[i], place) for i in range(2)]
-    spread_rows = [RingGather(normed.at[i], z_sends.at[2 + i], z_recvs.at[2 + i], place) for i in range(2)]
-    scatter_two = [
-        RingScatter(mixed.at[i], ring_two.at[i], z_sends.at[4 + i], z_recvs.at[4 + i], place) for i in range(2)
-    ]
+    rings = [(z_sends.at[i], z_recvs.at[i], place, 1 - 2 * (i % 2)) for i in range(6)]
+    scatter_one = [RingScatter(terms.at[i], ring_one.at[i], *rings[i]) for i in range(2)]
+    spread_rows = [RingGather(normed.at[i], *rings[2 + i]) for i in range(2)]
+    scatter_two = [RingScatter(mixed.at[i], ring_two.at[i], *rings[4 + i]) for i in range(2)]
 
     early, late = start_of(0), start_of(1)
     for gather in heads:
@@ -346,36 +349,30 @@
         gather.arrive(4)
         gather.start(6, 9)
     for gather in heads:
-        gather.arrive(8)
-    early = visit(early, 1)
-    for gather in heads:
-        gather.arrive(9)
-    early = visit(early, 2)
+        gather.arrive(8, 9)
+    early = visit(visit(early, 1), 2)
     for gather in heads:
         gather.arrive(5, 6)
         gather.start(10)
     for gather in experts:
         gather.start(0, 1, 2)
+    late = visit(late, 1)
     for gather in heads:
         gather.arrive(10)
     early = end_of(visit(early, 3))
     project(0, early)
     scatter_one[0].begin()
-    late = visit(late, 1)
-    late = visit(late, 2)
-    late = end_of(visit(late, 3))
+    late = end_of(visit(visit(late, 2), 3))
     project(1, late)
     scatter_one[1].begin()
     pair = [rows.reshape(RING, PART, 2 * HEAD_SIZE) for rows in (early, late)]
     attn_v[...] = jnp.concatenate(pair, axis=1).reshape(TOKENS, 2 * HEAD_SIZE).astype(BF16)
     attn_copy = pltpu.make_async_copy(attn_v, attn_out, loads.at[len(pairs)])
     attn_copy.start()
-    scatter_one[0].relay(3)
     for gather in experts:
         gather.arrive(0, 1, 2)
         gather.start(3, 4, 7)
-    scatter_one[1].relay(3)
-    for step in (2, 1):
+    for step in (3, 2, 1):
         for part in range(2):
             scatter_one[part].relay(step)
     hidden = []

time: 103 us -> 99.3 us (0.964); the launches traced: 102 us -> 99.2 us
  Pallas kernels: 98.6 us -> 96.3 us
    pallas_call x1, Pallas kernels: 98.6 us -> 96.3 us  [local_layer(): pl.pallas_call(layer, out_shape=(jax.ShapeDtypeStruct(queries.shape, BF16...]
where the time goes in v4:
time: 99.3 us; the launch traced here: 99.2 us
  Pallas kernels  96.3 us (97%)
  local copies, waits for them, and re-layouts  2.23 us (2%)
    pallas_call x1, Pallas kernels, local_layer(): pl.pallas_call(layer, out_shape=(jax.ShapeDtypeStruct(queries.shape, BF16...  96.3 us
    unnamed x4, local copies, waits for them, and re-layouts  2.23 us

profile of v4, /device:TPU:6, one launch (start us, length us, event | category | flops | bytes accessed | tf_op | source)
XLA Modules:
  0.0 99.2 jit_solution(18057242037282101497)
XLA Ops:
  0.6 96.3 %layer.1 = (bf16[256,256]{1,0:T(8,128)(2,1)}, bf16[16,2048]{1,0:T(8,128)(2,1)}) custom-call(bf16[256,256]{1,0:T(8,128)(2,1)} %queries.1, bf16[256,512]{1,0:T(8,128)(2,1)} %keys.1, bf16[256,512]{1,0:T(8,128)(2,1)} %values.1, bf16[256,2048]{1,0:T(8,128)(2,1)} %out_proj.1, bf16[256,2048]{1,0:T(8,128)(2,1)} %resid.1, f32[1,2048]{1,0:T(1,128)} %bitcast.11, ...), custom_call_target="tpu_custom_call" | custom-call | tf_op jit(solution)/shard_map/layer/pallas_call | solution.py:425
  97.0 0.0 copy-start
  97.0 1.6 %copy.15 = bf16[256,256]{1,0:T(8,128)(2,1)} copy(bf16[256,256]{1,0:T(8,128)(2,1)} %get-tuple-element.4) | data formatting | bytes 262144
  98.6 0.0 copy-done
  98.6 0.6 copy.16
Async XLA Ops:
  97.0 1.6 %copy-start = (bf16[16,2048]{1,0:T(8,128)(2,1)S(1)}, bf16[16,2048]{1,0:T(8,128)(2,1)}, u32[]{:S(2)}) copy-start(bf16[16,2048]{1,0:T(8,128)(2,1)} %get-tuple-element.5) | copy-start | bytes 196612

commit v5 on v4

--- a/solution.py
+++ b/solution.py
@@ -102,11 +102,11 @@
         return total
 
     def relay(self, step):
+        self.lend(step - 1)
         for way in range(2):
             total = self.arrived(way, step) + self.term(way, 2 * step)[...].astype(F32)
             self.ring[way, 1, step] = total.astype(BF16)
             self.copy(way, 1, step - 1, self.ring.at[way, 1, step]).start()
-        self.lend(step - 1)
 
     def total(self):
         return self.terms[self.place].astype(F32) + self.arrived(0, 0) + self.arrived(1, 0)
@@ -221,7 +221,7 @@
         (gates, gates_v),
     ]
     local = [pltpu.make_async_copy(src, dst, loads.at[i]) for i, (src, dst) in enumerate(pairs)]
-    for copy in local:
+    for copy in local[:4]:
         copy.start()
 
     barrier = pltpu.get_barrier_semaphore()
@@ -242,6 +242,8 @@
         local[2 * index].wait()
         local[2 * index + 1].wait()
         gather.start(0, 1, 2)
+    for copy in local[4:]:
+        copy.start()
     for copy in local[4:]:
         copy.wait()
 

time: 99.3 us -> 99 us (level)
  no operation moved by 1% of the time
where the time goes in v5:
time: 99 us; the launch traced here: 98.8 us
  Pallas kernels  95.9 us (97%)
  local copies, waits for them, and re-layouts  2.23 us (2%)
    pallas_call x1, Pallas kernels, local_layer(): pl.pallas_call(layer, out_shape=(jax.ShapeDtypeStruct(queries.shape, BF16...  95.9 us
    unnamed x4, local copies, waits for them, and re-layouts  2.23 us

profile of v5, /device:TPU:6, one launch (start us, length us, event | category | flops | bytes accessed | tf_op | source)
XLA Modules:
  0.0 98.8 jit_solution(320140189795189295)
XLA Ops:
  0.6 95.9 %layer.1 = (bf16[256,256]{1,0:T(8,128)(2,1)}, bf16[16,2048]{1,0:T(8,128)(2,1)}) custom-call(bf16[256,256]{1,0:T(8,128)(2,1)} %queries.1, bf16[256,512]{1,0:T(8,128)(2,1)} %keys.1, bf16[256,512]{1,0:T(8,128)(2,1)} %values.1, bf16[256,2048]{1,0:T(8,128)(2,1)} %out_proj.1, bf16[256,2048]{1,0:T(8,128)(2,1)} %resid.1, f32[1,2048]{1,0:T(1,128)} %bitcast.11, ...), custom_call_target="tpu_custom_call" | custom-call | tf_op jit(solution)/shard_map/layer/pallas_call | solution.py:427
  96.6 0.0 copy-start
  96.6 1.6 %copy.15 = bf16[256,256]{1,0:T(8,128)(2,1)} copy(bf16[256,256]{1,0:T(8,128)(2,1)} %get-tuple-element.4) | data formatting | bytes 262144
  98.2 0.0 copy-done
  98.2 0.6 copy.16
Async XLA Ops:
  96.6 1.6 %copy-start = (bf16[16,2048]{1,0:T(8,128)(2,1)S(1)}, bf16[16,2048]{1,0:T(8,128)(2,1)}, u32[]{:S(2)}) copy-start(bf16[16,2048]{1,0:T(8,128)(2,1)} %get-tuple-element.5) | copy-start | bytes 196612
